TPU v7x, 32 devices: a whole 2x2x4 slice. The times are simulated.
32 devices in a mesh: groups: 2 (over y), samples: 8 (over z, x), features: 2 (over core).
Axes of the slice: x: 2, y: 2, z: 4, core: 2. Of those that a mesh axis runs over, the one named last changes fastest.
Arguments:
- blocks: bfloat16 [720, 8, 128, 128], P(('groups', 'samples'), 'features'), parts along dimension 0, may hold values from -0.15625 to 0.15625
- block_cols: int32 [720, 8], P(('groups', 'samples'), 'features'), parts along dimension 0, may hold values from 0 to 255, as said below
- right_side: float32 [65536, 128], P(('groups', 'samples', 'features')), parts along dimension 0, may hold values from -6 to 6
- lambdas: float32 [128], replicated, may hold values from 0.1 to 1.5
Outputs:
- solution: float32 [65536, 128], P(('groups', 'samples', 'features')), parts along dimension 0
- residual: float32 [65536, 128], P(('groups', 'samples', 'features')), parts along dimension 0
There are 2 independent parts, one for each index of `groups`. A program takes and returns all parts, laid end to end along the dimension named above; an argument that names none is the same for every part. Nothing has to cross between parts.
Inputs may be any that keep to these rules, and one draw needn't show every extreme that they name: `block_cols`: each row block names 8 distinct feature blocks; entries e < 4 name blocks g with (g // 16) % 2 == 0, the other entries blocks with (g // 16) % 2 == 1.
All inputs are finite; a program needn't handle non-finite values.
Results may differ from a plain program's by a relative error of at most 0.0087.
Values may be sent and summed in bfloat16 or wider, within the bound.
A program may use at most 128 MiB of HBM per device.

v0:
```python
import jax
import jax.numpy as jnp
from jax import lax
from jax.sharding import PartitionSpec as P

ITERS = 2


def local_tiles(block_cols, shard_blocks):
    return block_cols // (2 * shard_blocks) * shard_blocks + block_cols % shard_blocks


def normal_image(blocks, slot_ids, direction_panel):
    block_edge = blocks.shape[-1]
    target_width = direction_panel.shape[1]
    panel_tiles = direction_panel.reshape(-1, block_edge, target_width)
    picked = panel_tiles[slot_ids]
    partial_images = jnp.einsum(
        "reij,rejk->rik", blocks, picked, preferred_element_type=jnp.float32
    )
    images_full = lax.psum(partial_images, "features")
    narrow = images_full.astype(jnp.bfloat16)
    back_terms = jnp.einsum("reij,rik->rejk", blocks, narrow, preferred_element_type=jnp.float32)
    owner_sums = jax.ops.segment_sum(
        back_terms.reshape(-1, block_edge, target_width),
        slot_ids.reshape(-1),
        num_segments=panel_tiles.shape[0],
    )
    return owner_sums.reshape(direction_panel.shape[0], target_width)


def all_norm(residual):
    return lax.psum(jnp.sum(residual * residual, axis=0), ("samples", "features"))


def per_device(blocks, block_cols, right_side, lambdas):
    block_edge = blocks.shape[-1]
    shard_blocks = right_side.shape[0] // block_edge
    slot_ids = local_tiles(block_cols, shard_blocks)
    solution = jnp.zeros_like(right_side)
    residual = right_side
    direction = right_side
    norm_now = all_norm(residual)
    for iteration in range(ITERS):
        direction_panel = lax.all_gather(
            direction.astype(jnp.bfloat16), "samples", axis=0, tiled=True
        )
        owner_sums = normal_image(blocks, slot_ids, direction_panel)
        image = (
            lax.psum_scatter(owner_sums, "samples", scatter_dimension=0, tiled=True)
            + lambdas[None, :] * direction
        )
        curvature = lax.psum(jnp.sum(direction * image, axis=0), ("samples", "features"))
        step_size = norm_now / curvature
        solution = solution + step_size[None, :] * direction
        residual = residual - step_size[None, :] * image
        norm_next = all_norm(residual)
        direction = residual + (norm_next / norm_now)[None, :] * direction
        norm_now = norm_next
    return (solution, residual)


def solution(mesh):
    in_specs = (
        P(("groups", "samples"), "features", None, None),
        P(("groups", "samples"), "features"),
        P(("groups", "samples", "features"), None),
        P(),
    )
    out_specs = (
        P(("groups", "samples", "features"), None),
        P(("groups", "samples", "features"), None),
    )
    return jax.shard_map(
        per_device, mesh=mesh, in_specs=in_specs, out_specs=out_specs, check_vma=False
    )
```

profile of v0, /device:TPU:0, one launch (start us, length us, event | category | flops | bytes accessed | tf_op | source)
XLA Modules:
  0.0 749.8 jit_solution(865599778677976963)
XLA Ops:
  7.2 0.0 all-gather.3.cloned.1.call-start
  7.2 2.1 convert_element_type.12
  9.3 0.0 all-gather.3.cloned.1.call-update
  9.3 0.0 reduce-scatter.3.cloned.1.call-start
  9.4 0.7 compare_select_fusion
  10.1 0.1 copy.7
  10.2 0.1 reshape.34
  10.3 0.1 copy.6
  10.4 0.1 reshape.50
  10.5 76.3 %all-gather.3.cloned.1.call-done = bf16[16384,128]{1,0:T(8,128)(2,1)} async-done(((bf16[2048,128]{1,0:T(8,128)(2,1)}), bf16[16384,128]{1,0:T(8,128)(2,1)}) %all-gather.3.cloned.1.call-update) | async-done | bytes 4194320 | tf_op jit(solution)/shard_map/all_gather | solution.py:45
  86.8 10.1 %gather_fusion = bf16[180,128,128]{2,1,0:T(8,128)(2,1)} fusion(bf16[128,128,128]{2,1,0:T(8,128)(2,1)} %bitcast.44, s32[1024]{0:T(1024)S(1)} %pad_clamp_fusion), kind=kCustom, calls=%fused_computation | custom fusion | bytes 11797200 | tf_op jit(solution)/shard_map/gather | solution.py:17
  96.9 7.8 %convolution_bitcast_fusion.1 = f32[45,128,128]{1,2,0:T(8,128)} fusion(bf16[45,4,128,128]{3,2,1,0:T(8,128)(2,1)} %bitcast.43, bf16[45,4,128,128]{3,2,1,0:T(8,128)(2,1)} %param.4), kind=kOutput, calls=%fused_computation.5 | convolution fusion | flops 754974720 | bytes 14745600 | tf_op jit(solution)/shard_map/reij,rejk->rik/dot_general | solution.py:18
  104.7 11.6 %all-reduce.3 = bf16[45,128,128]{1,2,0:T(8,128)(2,1)S(1)} all-reduce(f32[45,128,128]{1,2,0:T(8,128)} %convolution_bitcast_fusion.1), channel_id=1, replica_groups=mesh['groups'=2,'samples'=8,'features'=2] {'features'}, use_global_device_ids=true, to_apply=%region_2.3 | all-reduce | flops 737280 | bytes 4423680 | tf_op jit(solution)/shard_map/psum | solution.py:21
  116.4 8.6 %fusion.2 = f32[45,128,4,128]{3,1,2,0:T(8,128)} fusion(bf16[45,4,128,128]{3,2,1,0:T(8,128)(2,1)} %param.4, bf16[45,128,128]{1,2,0:T(8,128)(2,1)S(1)} %all-reduce.3), kind=kOutput, calls=%fused_computation.8 | convolution fusion | flops 754974720 | bytes 19169280 | tf_op jit(solution)/shard_map/reij,rik->rejk/dot_general | solution.py:23
  125.0 12.3 %copy.8 = f32[180,128,128]{2,1,0:T(8,128)} copy(f32[180,128,128]{1,2,0:T(8,128)} %bitcast.40) | data formatting | bytes 23592960 | tf_op jit(solution)/shard_map/reshape | solution.py:25
  137.3 4.3 broadcast.22.clone
  141.6 39.4 %scatter_fusion = f32[128,128,128]{2,1,0:T(8,128)} fusion(f32[128,128,128]{2,1,0:T(8,128)} %broadcast.22.clone, s32[180]{0:T(256)S(1)} %reshape.50, f32[180,128,128]{2,1,0:T(8,128)} %copy.8), kind=kCustom, calls=%fused_computation.2 | custom fusion | flops 2949120 | bytes 35390160 | tf_op jit(solution)/shard_map/scatter-add | solution.py:24
  181.0 0.0 copy-start
  181.0 0.0 copy-start.2
  181.0 0.0 reduce-scatter.3.cloned.1.call-update
  181.0 0.0 all-gather.5.cloned.1.call-start
  181.1 147.3 %reduce-scatter.3.cloned.1.call-done = f32[2048,128]{1,0:T(8,128)} async-done(((f32[16384,128]{1,0:T(8,128)}), f32[2048,128]{1,0:T(8,128)}) %reduce-scatter.3.cloned.1.call-update) | async-done | bytes 1048592 | tf_op jit(solution)/shard_map/reduce_scatter | solution.py:50
  328.4 0.0 copy-done
  328.4 0.0 copy-done.2
  328.4 1.5 multiply_reduce_fusion.2
  329.9 31.5 %all-reduce = (f32[128]{0:T(128)S(1)}, f32[128]{0:T(128)S(1)}) all-reduce(f32[128]{0:T(128)S(1)} %get-tuple-element.3, f32[128]{0:T(128)S(1)} %get-tuple-element.2), channel_id=1, replica_groups=mesh['groups'=2,'samples'=8,'features'=2] {'samples','features'}, use_global_device_ids=true, to_apply=%region_1.2 | all-reduce | flops 256 | bytes 2048 | tf_op jit(solution)/shard_map/psum | solution.py:33
  361.4 1.5 multiply_reduce_fusion.1
  362.9 29.5 %psum.45 = f32[128]{0:T(128)S(1)} all-reduce(f32[128]{0:T(128)S(1)} %multiply_reduce_fusion.1), channel_id=1, replica_groups=mesh['groups'=2,'samples'=8,'features'=2] {'samples','features'}, use_global_device_ids=true, to_apply=%region_8.9 | all-reduce | flops 128 | bytes 1024 | tf_op jit(solution)/shard_map/psum | solution.py:33
  392.4 2.3 fusion.6
  394.7 0.0 all-gather.5.cloned.1.call-update
  394.7 0.2 reduce-scatter.5.cloned.1.call-start
  395.0 70.6 %all-gather.5.cloned.1.call-done = bf16[16384,128]{1,0:T(8,128)(2,1)} async-done(((bf16[2048,128]{1,0:T(8,128)(2,1)}), bf16[16384,128]{1,0:T(8,128)(2,1)}) %all-gather.5.cloned.1.call-update) | async-done | bytes 4194320 | tf_op jit(solution)/shard_map/all_gather | solution.py:45
  465.5 10.1 %gather_fusion.1 = bf16[180,128,128]{2,1,0:T(8,128)(2,1)} fusion(bf16[128,128,128]{2,1,0:T(8,128)(2,1)} %bitcast.45, s32[1024]{0:T(1024)S(1)} %pad_clamp_fusion), kind=kCustom, calls=%fused_computation.1 | custom fusion | bytes 11797200 | tf_op jit(solution)/shard_map/gather | solution.py:17
  475.6 7.8 %convolution_bitcast_fusion = f32[45,128,128]{1,2,0:T(8,128)} fusion(bf16[45,4,128,128]{3,2,1,0:T(8,128)(2,1)} %bitcast.42, bf16[45,4,128,128]{3,2,1,0:T(8,128)(2,1)} %param.4), kind=kOutput, calls=%fused_computation.4 | convolution fusion | flops 754974720 | bytes 14745600 | tf_op jit(solution)/shard_map/reij,rejk->rik/dot_general | solution.py:18
  483.4 11.6 %all-reduce.4 = bf16[45,128,128]{1,2,0:T(8,128)(2,1)S(1)} all-reduce(f32[45,128,128]{1,2,0:T(8,128)} %convolution_bitcast_fusion), channel_id=1, replica_groups=mesh['groups'=2,'samples'=8,'features'=2] {'features'}, use_global_device_ids=true, to_apply=%region_9.10 | all-reduce | flops 737280 | bytes 4423680 | tf_op jit(solution)/shard_map/psum | solution.py:21
  495.1 8.6 %fusion = f32[45,128,4,128]{3,1,2,0:T(8,128)} fusion(bf16[45,4,128,128]{3,2,1,0:T(8,128)(2,1)} %param.4, bf16[45,128,128]{1,2,0:T(8,128)(2,1)S(1)} %all-reduce.4), kind=kOutput, calls=%fused_computation.6 | convolution fusion | flops 754974720 | bytes 19169280 | tf_op jit(solution)/shard_map/reij,rik->rejk/dot_general | solution.py:23
  503.7 12.3 %copy.9 = f32[180,128,128]{2,1,0:T(8,128)} copy(f32[180,128,128]{1,2,0:T(8,128)} %bitcast.41) | data formatting | bytes 23592960 | tf_op jit(solution)/shard_map/reshape | solution.py:25
  515.9 4.3 broadcast.22
  520.2 39.4 %scatter_fusion.1 = f32[128,128,128]{2,1,0:T(8,128)} fusion(f32[128,128,128]{2,1,0:T(8,128)} %broadcast.22, s32[180]{0:T(256)S(1)} %reshape.50, f32[180,128,128]{2,1,0:T(8,128)} %copy.9), kind=kCustom, calls=%fused_computation.3 | custom fusion | flops 2949120 | bytes 35390160 | tf_op jit(solution)/shard_map/scatter-add | solution.py:24
  559.7 0.0 copy-start.1
  559.7 0.0 reduce-scatter.5.cloned.1.call-update
  559.7 147.4 %reduce-scatter.5.cloned.1.call-done = f32[2048,128]{1,0:T(8,128)} async-done(((f32[16384,128]{1,0:T(8,128)}), f32[2048,128]{1,0:T(8,128)}) %reduce-scatter.5.cloned.1.call-update) | async-done | bytes 1048592 | tf_op jit(solution)/shard_map/reduce_scatter | solution.py:50
  707.1 0.0 copy-done.1
  707.1 1.6 multiply_reduce_fusion
  708.7 31.5 %psum.47 = f32[128]{0:T(128)S(1)} all-reduce(f32[128]{0:T(128)S(1)} %multiply_reduce_fusion), channel_id=1, replica_groups=mesh['groups'=2,'samples'=8,'features'=2] {'samples','features'}, use_global_device_ids=true, to_apply=%region_13.14 | all-reduce | flops 128 | bytes 1024 | tf_op jit(solution)/shard_map/psum | solution.py:53
  740.2 3.0 multiply_subtract_fusion
  (4 shorter events, 0.0 us)
Async XLA Ops:
  7.2 79.7 %all-gather.3.cloned.1.call-start = ((), (), s32[]{:S(2)}) async-start(), calls=%async_computation.2 | async-start | bytes 4718592 | tf_op jit(solution)/shard_map/all_gather | solution.py:45
  9.3 319.1 %reduce-scatter.3.cloned.1.call-start = ((), (), s32[]{:S(2)}) async-start(), calls=%async_computation.3 | async-start | bytes 9437184 | tf_op jit(solution)/shard_map/reduce_scatter | solution.py:50
  181.0 147.4 %copy-start = (f32[2048,128]{1,0:T(8,128)S(1)}, f32[2048,128]{1,0:T(8,128)}, u32[]{:S(2)}) copy-start(f32[2048,128]{1,0:T(8,128)} %param.6) | copy-start | bytes 3145732
  181.0 147.4 %copy-start.2 = (f32[128]{0:T(128)S(1)}, f32[128]{0:T(128)}, u32[]{:S(2)}) copy-start(f32[128]{0:T(128)} %param.7) | copy-start | bytes 1540
  181.0 284.5 %all-gather.5.cloned.1.call-start = ((), (), s32[]{:S(2)}) async-start(), calls=%async_computation.4 | async-start | bytes 4718592 | tf_op jit(solution)/shard_map/all_gather | solution.py:45
  394.7 312.4 %reduce-scatter.5.cloned.1.call-start = ((), (), s32[]{:S(2)}) async-start(), calls=%async_computation.5 | async-start | bytes 9437184 | tf_op jit(solution)/shard_map/reduce_scatter | solution.py:50
  559.7 147.4 %copy-start.1 = (f32[2048,128]{1,0:T(8,128)S(1)}, f32[2048,128]{1,0:T(8,128)}, u32[]{:S(2)}) copy-start(f32[2048,128]{1,0:T(8,128)} %reduce-scatter.3.cloned.1.call-done) | copy-start | bytes 3145732
Sparse Core Ops, SparseCore 0:
  10.7 76.0 all-gather.2
  181.1 147.2 reduce-scatter.2
  394.8 70.6 all-gather.4
  559.8 147.2 reduce-scatter.4
where the time goes:
time: 752 us; the launch traced here: 750 us
  waiting for transfers between devices  442 us (59%)
  blocking collectives  116 us (15%)
  other arithmetic  91.5 us (12%)
  local copies, waits for them, and re-layouts  53.7 us (7%)
  matrix products  32.9 us (4%)
  between operations  13.8 us (2%)
    reduce_scatter x2, waiting for transfers between devices, per_device(): lax.psum_scatter(owner_sums, 'samples', scatter_dimension=0, tiled=True)  295 us
    all_gather x2, waiting for transfers between devices, per_device(): lax.all_gather(direction.astype(jnp.bfloat16), 'samples', axis=0, tiled=T...  147 us
    scatter-add x2, other arithmetic, normal_image(): jax.ops.segment_sum(back_terms.reshape(-1, block_edge, target_width), slo...  78.9 us
    psum x2, blocking collectives, all_norm(): lax.psum(jnp.sum(residual * residual, axis=0), ('samples', 'features'))  61 us
    psum x1, blocking collectives, per_device(): lax.psum(jnp.sum(direction * image, axis=0), ('samples', 'features'))  31.5 us
    reshape x2, local copies, waits for them, and re-layouts, normal_image(): back_terms.reshape(-1, block_edge, target_width)  24.5 us
    psum x2, blocking collectives, normal_image(): images_full = lax.psum(partial_images, 'features')  23.2 us
    gather x2, local copies, waits for them, and re-layouts, normal_image(): picked = panel_tiles[slot_ids]  20.2 us
  transfers between devices with their start and end apart: 4, of which 4 were waited for; matrix products, arithmetic and copies ran while one was open for 0% of the time, Pallas kernels for 0%

commit v1 on v0

v1 whole, which is shorter than its diff:
```python
import functools

import jax
import jax.numpy as jnp
from jax import lax
from jax.experimental import pallas as pl
from jax.experimental.pallas import tpu as pltpu
from jax.sharding import PartitionSpec as P

ITERS = 2
MESH = pl.DeviceIdType.MESH
F32 = jnp.float32
BF16 = jnp.bfloat16


def row_length(n):
    return 1 << ((n.bit_length() - 1) // 3)


def fold(a):
    return jnp.sum(a.reshape(-1, 8, a.shape[-1]), axis=0)


def kernel(
    n, X, SB,
    slots, prev, last, blocks_hbm, right, lam,
    sol, res,
    blocks, panel, img, imr, low, chain, acc, xs, xr, zs, zr, p, q,
    core_buf, all_buf,
    blk_sem, agz_s, agz_r, agx_s, agx_r, ft_s, ft_r, rsx_s, rsx_r, rsz_s, rsz_r,
    co_s, co_r, ar_s, ar_r,
):
    Z = n // X
    RB, E = blocks.shape[0], blocks.shape[1]
    CH = RB // img_chunks(RB)
    me = lax.axis_index("samples")
    core = lax.axis_index("features")
    z, x = me // X, me % X

    load = pltpu.make_async_copy(blocks_hbm, blocks, blk_sem)
    load.start()

    barrier = pltpu.get_barrier_semaphore()
    pl.semaphore_signal(barrier, inc=1, device_id={"features": 1 - core}, device_id_type=MESH)

    @pl.loop(1, n)
    def _(d):
        pl.semaphore_signal(
            barrier, inc=1, device_id={"samples": (me + d) % n}, device_id_type=MESH
        )

    def to(src, dst, ss, rs, **where):
        return pltpu.make_async_remote_copy(
            src_ref=src, dst_ref=dst, send_sem=ss, recv_sem=rs,
            device_id=where, device_id_type=MESH,
        )

    def shard(t, xx):
        return panel.at[pl.ds((t * X + xx) * SB, SB)]

    def gather(it):
        def zcopy(t, d):
            return to(shard(t, x), shard(t, x), agz_s.at[it, d, t], agz_r.at[it, t],
                      samples=me + (X if d == 0 else -X))

        def xcopy(t, dx, src_x):
            return to(shard(t, src_x), shard(t, src_x), agx_s.at[it, dx - 1, t],
                      agx_r.at[it, dx - 1, t], samples=z * X + (x + dx) % X)

        def send_x(t):
            for dx in range(1, X):
                xcopy(t, dx, x).start()

        for k in range(Z):
            for d in (0, 1):
                if k == 0 and d == 1:
                    continue
                t = z - k if d == 0 else z + k
                ok = (t >= 0) if d == 0 else (t < Z)

                def step(t=t, d=d):
                    if k:
                        zcopy(t, d).wait_recv()
                    for dd in ((0, 1) if k == 0 else (d,)):
                        pl.when((z + 1 < Z) if dd == 0 else (z > 0))(
                            lambda dd=dd: zcopy(t, dd).start())
                    send_x(t)

                if k:
                    pl.when(ok)(step)
                else:
                    step()
        for t in range(Z):
            for dx in range(1, X):
                xcopy(t, dx, (x - dx + X) % X).wait_recv()
        for t in range(Z):
            for dx in range(1, X):
                xcopy(t, dx, x).wait_send()
            pl.when((t <= z) & (z + 1 < Z))(lambda t=t: zcopy(t, 0).wait_send())
            pl.when((t >= z) & (z > 0))(lambda t=t: zcopy(t, 1).wait_send())

    def products(it):
        def part(c):
            rows = pl.ds(c * CH, CH)
            return to(img.at[rows], imr.at[rows], ft_s.at[it, c], ft_r.at[it, c],
                      features=1 - core)

        for c in range(RB // CH):
            @pl.loop(c * CH, (c + 1) * CH)
            def _(r):
                lhs = jnp.concatenate([blocks[r, e] for e in range(E)], axis=1)
                rhs = jnp.concatenate([panel[slots[r * E + e]] for e in range(E)], axis=0)
                img[r] = jnp.dot(lhs, rhs, preferred_element_type=F32)

            part(c).start()
        for c in range(RB // CH):
            part(c).wait_recv()

            @pl.loop(c * CH, (c + 1) * CH)
            def _(r):
                narrow = (img[r] + imr[r]).astype(BF16)
                for e in range(E):
                    term = lax.dot_general(
                        blocks[r, e], narrow, (((0,), (0,)), ((), ())),
                        preferred_element_type=F32)
                    i = r * E + e
                    chain[i + 1] = term + chain[prev[i]]

        for c in range(RB // CH):
            part(c).wait_send()

    def scatter(it):
        def xcopy(t, dx):
            return to(xs.at[dx - 1, t], xr.at[dx - 1, t], rsx_s.at[it, dx - 1, t],
                      rsx_r.at[it, dx - 1, t], samples=z * X + (x + dx) % X)

        def zcopy(t, d):
            return to(zs.at[t], zr.at[d, t], rsz_s.at[it, t], rsz_r.at[it, d, t],
                      samples=me + X - 2 * X * d)

        order = []
        a, b = z * 0, z * 0 + Z - 1
        for k in range(Z):
            low_end = (z - a > b - z).astype(jnp.int32)
            order.append(a * low_end + b * (1 - low_end))
            a = a + low_end
            b = b - (1 - low_end)

        for t in order:
            for dx in range(1, X):
                base = (t * X + (x + dx) % X) * SB

                @pl.loop(0, SB)
                def _(w):
                    xs[dx - 1, t, w] = chain[last[base + w]].astype(BF16)

                xcopy(t, dx).start()
        for t in order:
            base = (t * X + x) * SB

            @pl.loop(0, SB)
            def _(w):
                acc[t, w] = chain[last[base + w]]

        for k, t in enumerate(order):
            for dx in range(1, X):
                xcopy(t, dx).wait_recv()

            if k < Z - 1:
                d = (t < z).astype(jnp.int32)
                relay = ((t > z) & (z > 0)) | ((t < z) & (z + 1 < Z))
                pl.when(relay)(lambda: zcopy(t, d).wait_recv())
                more = relay.astype(jnp.int32)

                @pl.when(relay)
                def _():
                    @pl.loop(0, SB)
                    def _(w):
                        total = acc[t, w] + zr[d, t, w].astype(F32)
                        for dx in range(1, X):
                            total = total + xr[dx - 1, t, w].astype(F32)
                        zs[t, w] = total.astype(BF16)

                @pl.when(more == 0)
                def _():
                    @pl.loop(0, SB)
                    def _(w):
                        total = acc[t, w]
                        for dx in range(1, X):
                            total = total + xr[dx - 1, t, w].astype(F32)
                        zs[t, w] = total.astype(BF16)

                zcopy(t, d).start()
            else:
                @pl.loop(0, SB)
                def _(w):
                    total = acc[z, w]
                    for dx in range(1, X):
                        total = total + xr[dx - 1, z, w].astype(F32)
                    q[w] = total

        def arrive(d):
            zcopy(z, d).wait_recv()

            @pl.loop(0, SB)
            def _(w):
                q[w] = q[w] + zr[d, z, w].astype(F32)

        pl.when(z > 0)(lambda: arrive(0))
        pl.when(z + 1 < Z)(lambda: arrive(1))
        for t in range(Z):
            for dx in range(1, X):
                xcopy(t, dx).wait_send()
            pl.when(t != z)(lambda t=t: zcopy(t, 0).wait_send())

    def all_sum(a, j, values):
        m = len(values)
        rows = pl.ds(0, 8 * m)
        for i, v in enumerate(values):
            core_buf[j, 0, pl.ds(8 * i, 8)] = v
        cc = to(core_buf.at[j, 0, rows], core_buf.at[j, 1, rows], co_s.at[j], co_r.at[j],
                features=1 - core)
        cc.start()
        cc.wait()
        all_buf[j, me, rows] = core_buf[j, 0, rows] + core_buf[j, 1, rows]

        def copy(d):
            return to(all_buf.at[j, me, rows], all_buf.at[j, me, rows], ar_s.at[j, d],
                      ar_r.at[j, d], samples=(me + d) % n)

        def incoming(d):
            src = (me - d + n) % n
            return to(all_buf.at[j, src, rows], all_buf.at[j, src, rows], ar_s.at[j, d],
                      ar_r.at[j, d], samples=(me + d) % n)

        @pl.loop(1, n)
        def _(d):
            copy(d).start()

        @pl.loop(1, n)
        def _(d):
            incoming(d).wait_recv()

        @pl.loop(1, n)
        def _(d):
            copy(d).wait_send()

        total = all_buf[j, 0, rows]
        for s in range(1, n):
            total = total + all_buf[j, s, rows]
        return [jnp.sum(total[8 * i:8 * i + 8], axis=0, keepdims=True) for i in range(m)]

    zero = jnp.zeros((8, right.shape[-1]), F32)
    for w in range(SB):
        panel[me * SB + w] = right[w].astype(BF16)
    pl.semaphore_wait(barrier, n)
    gather(0)
    chain[0] = jnp.zeros(chain.shape[1:], F32)
    load.wait()
    norm = None
    for it in range(ITERS):
        final = it == ITERS - 1
        direction = right if it == 0 else p
        residual = right if it == 0 else res
        products(it)
        scatter(it)

        def curve(w, carry):
            dot, sq = carry
            v = direction[w]
            image = q[w] + lam[...] * v
            q[w] = image
            return dot + fold(v * image), sq + fold(v * v)

        dot, sq = lax.fori_loop(0, SB, curve, (zero, zero))
        if it == 0:
            norm, curvature = all_sum(None, 0, [sq, dot])
        else:
            (curvature,) = all_sum(None, 2 * it, [dot])
        step = norm / curvature

        def update(w, carry):
            v = direction[w]
            sol[w] = step * v if it == 0 else sol[w] + step * v
            new = residual[w] - step * q[w]
            res[w] = new
            return carry + fold(new * new)

        sq = lax.fori_loop(0, SB, update, zero)
        if not final:
            (norm_next,) = all_sum(None, 2 * it + 1, [sq])
            ratio = norm_next / norm
            norm = norm_next

            @pl.loop(0, SB)
            def _(w):
                v = res[w] + ratio * direction[w]
                p[w] = v
                panel[me * SB + w] = v.astype(BF16)

            gather(it + 1)


def img_chunks(rb):
    return max(d for d in range(1, 6) if rb % d == 0)


def per_device(n, blocks, block_cols, right_side, lambdas):
    RB, E, B, _ = blocks.shape
    K = right_side.shape[1]
    SB = right_side.shape[0] // B
    X = row_length(n)
    Z = n // X
    slots = (block_cols // (2 * SB) * SB + block_cols % SB).reshape(-1)
    entries = jnp.arange(RB * E, dtype=jnp.int32)
    same = (slots[:, None] == slots[None, :]) & (entries[None, :] < entries[:, None])
    prev = jnp.max(jnp.where(same, entries[None, :] + 1, 0), axis=1)
    hit = slots[None, :] == jnp.arange(n * SB, dtype=jnp.int32)[:, None]
    last = jnp.max(jnp.where(hit, entries[None, :] + 1, 0), axis=1)
    C = img_chunks(RB)
    dma = pltpu.SemaphoreType.DMA
    J = 2 * ITERS
    smem = pl.BlockSpec(memory_space=pltpu.SMEM)
    vmem = pl.BlockSpec(memory_space=pltpu.VMEM)
    sol, res = pl.pallas_call(
        functools.partial(kernel, n, X, SB),
        out_shape=[jax.ShapeDtypeStruct((SB, B, K), F32)] * 2,
        in_specs=[smem, smem, smem, pl.BlockSpec(memory_space=pl.ANY), vmem, vmem],
        out_specs=[vmem, vmem],
        scratch_shapes=[
            pltpu.VMEM((RB, E, B, B), BF16),
            pltpu.VMEM((n * SB, B, K), BF16),
            pltpu.VMEM((RB, B, K), F32),
            pltpu.VMEM((RB, B, K), F32),
            pltpu.VMEM((1, 16, K), BF16),
            pltpu.VMEM((RB * E + 1, B, K), F32),
            pltpu.VMEM((Z, SB, B, K), F32),
            pltpu.VMEM((X - 1, Z, SB, B, K), BF16),
            pltpu.VMEM((X - 1, Z, SB, B, K), BF16),
            pltpu.VMEM((Z, SB, B, K), BF16),
            pltpu.VMEM((2, Z, SB, B, K), BF16),
            pltpu.VMEM((SB, B, K), F32),
            pltpu.VMEM((SB, B, K), F32),
            pltpu.VMEM((J, 2, 16, K), F32),
            pltpu.VMEM((J, n, 16, K), F32),
            dma,
            dma((ITERS, 2, Z)), dma((ITERS, Z)),
            dma((ITERS, X - 1, Z)), dma((ITERS, X - 1, Z)),
            dma((ITERS, C)), dma((ITERS, C)),
            dma((ITERS, X - 1, Z)), dma((ITERS, X - 1, Z)),
            dma((ITERS, Z)), dma((ITERS, 2, Z)),
            dma((J,)), dma((J,)), dma((J, n)), dma((J, n)),
        ],
        compiler_params=pltpu.CompilerParams(
            collective_id=0, has_side_effects=True, vmem_limit_bytes=60 * 2**20),
    )(slots, prev, last, blocks, right_side.reshape(SB, B, K), lambdas.reshape(1, K))
    return sol.reshape(right_side.shape), res.reshape(right_side.shape)


def solution(mesh):
    in_specs = (
        P(("groups", "samples"), "features", None, None),
        P(("groups", "samples"), "features"),
        P(("groups", "samples", "features"), None),
        P(),
    )
    out_specs = (
        P(("groups", "samples", "features"), None),
        P(("groups", "samples", "features"), None),
    )
    return jax.shard_map(
        functools.partial(per_device, mesh.shape["samples"]),
        mesh=mesh, in_specs=in_specs, out_specs=out_specs, check_vma=False,
    )
```

time: 752 us -> 257 us (0.34)
  waiting for transfers between devices: 442 us -> 0 us
  Pallas kernels: 0 us -> 249 us
  blocking collectives: 116 us -> 0 us
  other arithmetic: 91.5 us -> 2.1 us
  local copies, waits for them, and re-layouts: 53.7 us -> 4.74 us
  matrix products: 32.9 us -> 0 us
  between operations: 13.8 us -> 0.66 us
    reduce_scatter x2 -> x0, waiting for transfers between devices: 295 us -> none  [per_device(): lax.psum_scatter(owner_sums, 'samples', scatter_dimension=0, tiled=True)]
    pallas_call x0 -> x1, Pallas kernels: none -> 249 us  [per_device(): pl.pallas_call(functools.partial(kernel, n, X, SB), out_shape=[jax.ShapeD...]
    all_gather x2 -> x0, waiting for transfers between devices: 147 us -> none  [per_device(): lax.all_gather(direction.astype(jnp.bfloat16), 'samples', axis=0, tiled=T...]
    psum x5 -> x0, blocking collectives: 116 us -> none  [the longest x2 61 us: all_norm(): lax.psum(jnp.sum(residual * residual, axis=0), ('samples', 'features'))]
    scatter-add x2 -> x0, other arithmetic: 78.9 us -> none  [normal_image(): jax.ops.segment_sum(back_terms.reshape(-1, block_edge, target_width), slo...]
    dot_general x4 -> x0, matrix products: 32.9 us -> none  [the longest x2 17.3 us: normal_image(): jnp.einsum('reij,rik->rejk', blocks, narrow, preferred_element_type=jnp.f...]
    reshape x2 -> x1, local copies, waits for them, and re-layouts: 24.5 us -> 0.1 us  [per_device(): slots = (block_cols // (2 * SB) * SB + block_cols % SB).reshape(-1)]
    gather x2 -> x0, local copies, waits for them, and re-layouts: 20.2 us -> none  [normal_image(): picked = panel_tiles[slot_ids]]
  transfers between devices with their start and end apart: 4 -> 0, of which waited for: 4 -> 0; matrix products, arithmetic and copies ran while one was open for 0% -> 0% of each run, Pallas kernels for 0% -> 0%
where the time goes in v1:
time: 257 us; the launch traced here: 256 us
  Pallas kernels  249 us (97%)
  local copies, waits for them, and re-layouts  4.74 us (2%)
    pallas_call x1, Pallas kernels, per_device(): pl.pallas_call(functools.partial(kernel, n, X, SB), out_shape=[jax.ShapeD...  249 us

profile of v1, /device:TPU:0, one launch (start us, length us, event | category | flops | bytes accessed | tf_op | source)
XLA Modules:
  0.0 256.4 jit_solution(13371349112956333415)
XLA Ops:
  0.6 0.7 fusion.3
  1.3 0.1 copy.7
  1.4 0.1 reshape.26.slots
  1.5 0.0 copy-start
  1.6 0.6 select_reduce_fusion.1.last
  2.2 0.7 select_reduce_fusion.prev
  3.0 0.0 copy-done
  3.0 248.9 %shard_map.59 = (f32[16,128,128]{2,1,0:T(8,128)}, f32[16,128,128]{2,1,0:T(8,128)}) custom-call(s32[180]{0:T(256)} %copy-done, s32[180]{0:T(256)} %select_reduce_fusion.prev, s32[128]{0:T(128)} %select_reduce_fusion.1.last, bf16[45,4,128,128]{3,2,1,0:T(8,128)(2,1)} %blocks_hbm.1, f32[16,128,128]{2,1,0:T(8,128)} %bitcast.6, f32[1,128]{1,0:T(1,128)} %bitcast.7), custom_call_target="tpu_custom_call" | custom-call | tf_op jit(solution)/shard_map/pallas_call | solution.py:325
  251.8 2.3 copy.10
  254.1 2.3 copy.11
  (1 shorter events, 0.0 us)
Async XLA Ops:
  1.5 1.4 copy-start

commit v2 on v1

v2 whole, which is shorter than its diff:
```python
import functools

import jax
import jax.numpy as jnp
from jax import lax
from jax.experimental import pallas as pl
from jax.experimental.pallas import tpu as pltpu
from jax.sharding import PartitionSpec as P

ITERS = 2
MESH = pl.DeviceIdType.MESH
F32 = jnp.float32
BF16 = jnp.bfloat16


def row_length(n):
    return 1 << ((n.bit_length() - 1) // 3)


def fold(a):
    return jnp.sum(a.reshape(-1, 8, a.shape[-1]), axis=0)


def kernel(
    n, X, SB,
    slots, prev, last, blocks_hbm, right, lam,
    sol, res,
    blocks, panel, img, imr, chain, acc, xs, xr, zs, zr, es, er, p, q, all_buf,
    blk_sem, agz_s, agz_r, agx_s, agx_r, age_s, age_r, ft_s, ft_r,
    rsx_s, rsx_r, rsz_s, rsz_r, rse_s, rse_r, ar_s, ar_r,
):
    Z = n // X
    RB, E, B = blocks.shape[:3]
    CH = RB // img_chunks(RB)
    me = lax.axis_index("samples")
    core = lax.axis_index("features")
    z, x = me // X, me % X

    load = pltpu.make_async_copy(blocks_hbm, blocks, blk_sem)
    load.start()

    barrier = pltpu.get_barrier_semaphore()
    mine = me * 2 + core

    @pl.loop(1, 2 * n)
    def _(d):
        other = (mine + d) % (2 * n)
        pl.semaphore_signal(
            barrier, inc=1, device_id={"samples": other // 2, "features": other % 2},
            device_id_type=MESH)

    def to(src, dst, ss, rs, **where):
        return pltpu.make_async_remote_copy(
            src_ref=src, dst_ref=dst, send_sem=ss, recv_sem=rs,
            device_id=where, device_id_type=MESH,
        )

    HS = SB // 2
    zp = z + 1 - 2 * (z % 2)
    peer = me + X - 2 * X * (z % 2)

    def half(h):
        return pl.ds(h * HS, HS)

    def piece(t, xx, h):
        return panel.at[pl.ds((t * X + xx) * SB + h * HS, HS)]

    def gather(it):
        def zcopy(t, h, d):
            return to(piece(t, x, h), piece(t, x, h), agz_s.at[it, d, t, h],
                      agz_r.at[it, t, h], samples=me + (X if d == 0 else -X))

        def xcopy(t, h, dx, src_x):
            return to(piece(t, src_x, h), piece(t, src_x, h), agx_s.at[it, dx - 1, t, h],
                      agx_r.at[it, dx - 1, t, h], samples=z * X + (x + dx) % X)

        def ecopy(t, dx):
            ref = piece(t, (x - dx + X) % X, 1)
            return to(ref, ref, age_s.at[it, dx - 1], age_r.at[it, dx - 1], samples=peer)

        def send_x(t, h):
            for dx in range(1, X):
                xcopy(t, h, dx, x).start()

        for h in (0, 1):
            for d in (0, 1):
                pl.when((z + 1 < Z) if d == 0 else (z > 0))(
                    lambda h=h, d=d: zcopy(z, h, d).start())
            send_x(z, h)
        for k in range(1, Z):
            for h in (0, 1):
                for d in (0, 1):
                    t = z - k if d == 0 else z + k

                    @pl.when((t >= 0) if d == 0 else (t < Z))
                    def _(t=t, h=h, d=d, k=k):
                        zcopy(t, h, d).wait_recv()
                        pl.when((z + 1 < Z) if d == 0 else (z > 0))(
                            lambda: zcopy(t, h, d).start())
                        if k == 1 and h == 1:
                            pl.when(t != zp)(lambda: send_x(t, h))
                        else:
                            send_x(t, h)
            if k == 1:
                for dx in range(1, X):
                    xcopy(z, 1, dx, (x - dx + X) % X).wait_recv()
                    ecopy(z, dx).start()
        for t in range(Z):
            for dx in range(1, X):
                xcopy(t, 0, dx, (x - dx + X) % X).wait_recv()
                pl.when((t != zp) & (t != z))(
                    lambda t=t, dx=dx: xcopy(t, 1, dx, (x - dx + X) % X).wait_recv())
        for dx in range(1, X):
            ecopy(zp, dx).wait_recv()
        for t in range(Z):
            for dx in range(1, X):
                xcopy(t, 0, dx, x).wait_send()
                pl.when(t != zp)(lambda t=t, dx=dx: xcopy(t, 1, dx, x).wait_send())
            for h in (0, 1):
                pl.when((t <= z) & (z + 1 < Z))(lambda t=t, h=h: zcopy(t, h, 0).wait_send())
                pl.when((t >= z) & (z > 0))(lambda t=t, h=h: zcopy(t, h, 1).wait_send())
        for dx in range(1, X):
            ecopy(z, dx).wait_send()

    def products(it):
        def part(c):
            rows = pl.ds(c * CH, CH)
            return to(img.at[rows], imr.at[rows], ft_s.at[it, c], ft_r.at[it, c],
                      features=1 - core)

        U = 3 if CH % 3 == 0 else 1

        for c in range(RB // CH):
            @pl.loop(c * CH, (c + 1) * CH, step=U)
            def _(r0):
                for u in range(U):
                    r = r0 + u
                    lhs = jnp.concatenate([blocks[r, e] for e in range(E)], axis=1)
                    rhs = jnp.concatenate([panel[slots[r * E + e]] for e in range(E)], axis=0)
                    img[r] = jnp.dot(lhs, rhs, preferred_element_type=F32)

            part(c).start()
        for c in range(RB // CH):
            part(c).wait_recv()

            @pl.loop(c * CH, (c + 1) * CH, step=U)
            def _(r0):
                terms = []
                for u in range(U):
                    r = r0 + u
                    narrow = (img[r] + imr[r]).astype(BF16)
                    wide = jnp.concatenate([blocks[r, e] for e in range(E)], axis=1)
                    terms.append(lax.dot_general(
                        wide, narrow, (((0,), (0,)), ((), ())), preferred_element_type=F32))
                for u in range(U):
                    for e in range(E):
                        i = (r0 + u) * E + e
                        chain[i + 1] = terms[u][e * B:(e + 1) * B] + chain[prev[i]]

        for c in range(RB // CH):
            part(c).wait_send()

    def scatter(it):
        def xcopy(t, h, dx):
            return to(xs.at[dx - 1, t, half(h)], xr.at[dx - 1, t, half(h)],
                      rsx_s.at[it, dx - 1, t, h], rsx_r.at[it, dx - 1, t, h],
                      samples=z * X + (x + dx) % X)

        def zcopy(t, h, d):
            return to(zs.at[t, half(h)], zr.at[d, t, half(h)], rsz_s.at[it, t, h],
                      rsz_r.at[it, d, t, h], samples=me + X - 2 * X * d)

        def ecopy(dx):
            return to(es.at[dx - 1], er.at[dx - 1], rse_s.at[it, dx - 1],
                      rse_r.at[it, dx - 1], samples=peer)

        def term(t, xx, w):
            return chain[last[(t * X + xx) * SB + w]]

        order = []
        a, b = z * 0, z * 0 + Z - 1
        for k in range(Z):
            low_end = (z - a > b - z).astype(jnp.int32)
            order.append(a * low_end + b * (1 - low_end))
            a = a + low_end
            b = b - (1 - low_end)

        def send_x(t, h, dx, extra=False):
            xx = (x + dx) % X

            @pl.loop(0, HS)
            def _(v):
                w = v + h * HS
                total = term(t, xx, w)
                if extra:
                    total = total + er[dx - 1, v].astype(F32)
                xs[dx - 1, t, w] = total.astype(BF16)

            xcopy(t, h, dx).start()

        def send_extra():
            for dx in range(1, X):
                @pl.loop(0, HS)
                def _(v):
                    es[dx - 1, v] = term(zp, (x + dx) % X, v + HS).astype(BF16)

                ecopy(dx).start()

        for k, t in enumerate(order):
            for h in (0, 1):
                for dx in range(1, X):
                    if h == 0:
                        send_x(t, h, dx)
                    elif k < Z - 1:
                        pl.when(t != zp)(lambda t=t, dx=dx: send_x(t, 1, dx))
                    else:
                        ecopy(dx).wait_recv()
                        send_x(t, h, dx, True)
                if k == 0 and h == 0:
                    send_extra()
        for t in order:
            @pl.loop(0, SB)
            def _(w):
                acc[t, w] = term(t, x, w)

        def add_x(t, h):
            for dx in range(1, X):
                xcopy(t, h, dx).wait_recv()

            @pl.loop(h * HS, (h + 1) * HS)
            def _(w):
                total = acc[t, w]
                for dx in range(1, X):
                    total = total + xr[dx - 1, t, w].astype(F32)
                acc[t, w] = total

        def add_z(t, h, d):
            zcopy(t, h, d).wait_recv()

            @pl.loop(h * HS, (h + 1) * HS)
            def _(w):
                acc[t, w] = acc[t, w] + zr[d, t, w].astype(F32)

        for k, t in enumerate(order):
            for h in (0, 1):
                if h == 1 and k < Z - 1:
                    pl.when(t != zp)(lambda t=t: add_x(t, 1))
                else:
                    add_x(t, h)
                if k == Z - 1:
                    pl.when(z > 0)(lambda t=t, h=h: add_z(t, h, 0))
                    pl.when(z + 1 < Z)(lambda t=t, h=h: add_z(t, h, 1))
                    continue
                d = (t < z).astype(jnp.int32)
                relay = ((t > z) & (z > 0)) | ((t < z) & (z + 1 < Z))
                pl.when(relay)(lambda t=t, h=h, d=d: add_z(t, h, d))

                @pl.loop(h * HS, (h + 1) * HS)
                def _(w):
                    zs[t, w] = acc[t, w].astype(BF16)

                zcopy(t, h, d).start()
        for t in range(Z):
            for dx in range(1, X):
                xcopy(t, 0, dx).wait_send()
                pl.when(t != zp)(lambda t=t, dx=dx: xcopy(t, 1, dx).wait_send())
            for h in (0, 1):
                pl.when(t != z)(lambda t=t, h=h: zcopy(t, h, 0).wait_send())
        for dx in range(1, X):
            ecopy(dx).wait_send()

    def all_sum(j, values):
        m = len(values)
        rows = pl.ds(0, 8 * m)
        for i, v in enumerate(values):
            all_buf[j, mine, pl.ds(8 * i, 8)] = v

        def copy(d, src):
            other = (mine + d) % (2 * n)
            return to(all_buf.at[j, src, rows], all_buf.at[j, src, rows], ar_s.at[j, d],
                      ar_r.at[j, d], samples=other // 2, features=other % 2)

        @pl.loop(1, 2 * n)
        def _(d):
            copy(d, mine).start()

        @pl.loop(1, 2 * n)
        def _(d):
            copy(d, (mine - d + 2 * n) % (2 * n)).wait_recv()

        @pl.loop(1, 2 * n)
        def _(d):
            copy(d, mine).wait_send()

        total = all_buf[j, 0, rows]
        for s in range(1, 2 * n):
            total = total + all_buf[j, s, rows]
        return [jnp.sum(total[8 * i:8 * i + 8], axis=0, keepdims=True) for i in range(m)]

    zero = jnp.zeros((8, right.shape[-1]), F32)
    for w in range(SB):
        panel[me * SB + w] = right[w].astype(BF16)
    pl.semaphore_wait(barrier, 2 * n - 1)
    gather(0)
    chain[0] = jnp.zeros(chain.shape[1:], F32)
    load.wait()
    norm = None
    for it in range(ITERS):
        final = it == ITERS - 1
        direction = right if it == 0 else p
        residual = right if it == 0 else res
        products(it)
        scatter(it)

        def curve(w, carry):
            dot, sq = carry
            v = direction[w]
            image = acc[z, w] + lam[...] * v
            q[w] = image
            return dot + fold(v * image), sq + fold(v * v)

        dot, sq = lax.fori_loop(0, SB, curve, (zero, zero))
        if it == 0:
            norm, curvature = all_sum(0, [sq, dot])
        else:
            (curvature,) = all_sum(2 * it, [dot])
        step = norm / curvature

        def update(w, carry):
            v = direction[w]
            sol[w] = step * v if it == 0 else sol[w] + step * v
            new = residual[w] - step * q[w]
            res[w] = new
            return carry + fold(new * new)

        sq = lax.fori_loop(0, SB, update, zero)
        if not final:
            (norm_next,) = all_sum(2 * it + 1, [sq])
            ratio = norm_next / norm
            norm = norm_next

            @pl.loop(0, SB)
            def _(w):
                v = res[w] + ratio * direction[w]
                p[w] = v
                panel[me * SB + w] = v.astype(BF16)

            gather(it + 1)


def img_chunks(rb):
    return max(d for d in range(1, 6) if rb % d == 0)


def per_device(n, blocks, block_cols, right_side, lambdas):
    RB, E, B, _ = blocks.shape
    K = right_side.shape[1]
    SB = right_side.shape[0] // B
    X = row_length(n)
    Z = n // X
    slots = (block_cols // (2 * SB) * SB + block_cols % SB).reshape(-1)
    entries = jnp.arange(RB * E, dtype=jnp.int32)
    same = (slots[:, None] == slots[None, :]) & (entries[None, :] < entries[:, None])
    prev = jnp.max(jnp.where(same, entries[None, :] + 1, 0), axis=1)
    hit = slots[None, :] == jnp.arange(n * SB, dtype=jnp.int32)[:, None]
    last = jnp.max(jnp.where(hit, entries[None, :] + 1, 0), axis=1)
    C = img_chunks(RB)
    dma = pltpu.SemaphoreType.DMA
    J = 2 * ITERS
    smem = pl.BlockSpec(memory_space=pltpu.SMEM)
    vmem = pl.BlockSpec(memory_space=pltpu.VMEM)
    sol, res = pl.pallas_call(
        functools.partial(kernel, n, X, SB),
        out_shape=[jax.ShapeDtypeStruct((SB, B, K), F32)] * 2,
        in_specs=[smem, smem, smem, pl.BlockSpec(memory_space=pl.ANY), vmem, vmem],
        out_specs=[vmem, vmem],
        scratch_shapes=[
            pltpu.VMEM((RB, E, B, B), BF16),
            pltpu.VMEM((n * SB, B, K), BF16),
            pltpu.VMEM((RB, B, K), F32),
            pltpu.VMEM((RB, B, K), F32),
            pltpu.VMEM((RB * E + 1, B, K), F32),
            pltpu.VMEM((Z, SB, B, K), F32),
            pltpu.VMEM((X - 1, Z, SB, B, K), BF16),
            pltpu.VMEM((X - 1, Z, SB, B, K), BF16),
            pltpu.VMEM((Z, SB, B, K), BF16),
            pltpu.VMEM((2, Z, SB, B, K), BF16),
            pltpu.VMEM((X - 1, SB // 2, B, K), BF16),
            pltpu.VMEM((X - 1, SB // 2, B, K), BF16),
            pltpu.VMEM((SB, B, K), F32),
            pltpu.VMEM((SB, B, K), F32),
            pltpu.VMEM((J, 2 * n, 16, K), F32),
            dma,
            dma((ITERS, 2, Z, 2)), dma((ITERS, Z, 2)),
            dma((ITERS, X - 1, Z, 2)), dma((ITERS, X - 1, Z, 2)),
            dma((ITERS, X - 1)), dma((ITERS, X - 1)),
            dma((ITERS, C)), dma((ITERS, C)),
            dma((ITERS, X - 1, Z, 2)), dma((ITERS, X - 1, Z, 2)),
            dma((ITERS, Z, 2)), dma((ITERS, 2, Z, 2)),
            dma((ITERS, X - 1)), dma((ITERS, X - 1)),
            dma((J, 2 * n)), dma((J, 2 * n)),
        ],
        compiler_params=pltpu.CompilerParams(
            collective_id=0, has_side_effects=True, vmem_limit_bytes=60 * 2**20),
    )(slots, prev, last, blocks, right_side.reshape(SB, B, K), lambdas.reshape(1, K))
    return sol.reshape(right_side.shape), res.reshape(right_side.shape)


def solution(mesh):
    in_specs = (
        P(("groups", "samples"), "features", None, None),
        P(("groups", "samples"), "features"),
        P(("groups", "samples", "features"), None),
        P(),
    )
    out_specs = (
        P(("groups", "samples", "features"), None),
        P(("groups", "samples", "features"), None),
    )
    return jax.shard_map(
        functools.partial(per_device, mesh.shape["samples"]),
        mesh=mesh, in_specs=in_specs, out_specs=out_specs, check_vma=False,
    )
```

time: 257 us -> 232 us (0.903)
  Pallas kernels: 249 us -> 224 us
    pallas_call x1, Pallas kernels: 249 us -> 224 us  [per_device(): pl.pallas_call(functools.partial(kernel, n, X, SB), out_shape=[jax.ShapeD...]
where the time goes in v2:
time: 232 us
  Pallas kernels  224 us (97%)
  local copies, waits for them, and re-layouts  4.74 us (2%)
    pallas_call x1, Pallas kernels, per_device(): pl.pallas_call(functools.partial(kernel, n, X, SB), out_shape=[jax.ShapeD...  224 us

profile of v2, /device:TPU:0, one launch (start us, length us, event | category | flops | bytes accessed | tf_op | source)
XLA Modules:
  0.0 231.9 jit_solution(12466243207901668170)
XLA Ops:
  0.6 0.7 fusion.3
  1.3 0.1 copy.7
  1.4 0.1 reshape.26.slots
  1.5 0.0 copy-start
  1.6 0.6 select_reduce_fusion.1.last
  2.2 0.7 select_reduce_fusion.prev
  3.0 0.0 copy-done
  3.0 224.4 %shard_map.59 = (f32[16,128,128]{2,1,0:T(8,128)}, f32[16,128,128]{2,1,0:T(8,128)}) custom-call(s32[180]{0:T(256)} %copy-done, s32[180]{0:T(256)} %select_reduce_fusion.prev, s32[128]{0:T(128)} %select_reduce_fusion.1.last, bf16[45,4,128,128]{3,2,1,0:T(8,128)(2,1)} %blocks_hbm.1, f32[16,128,128]{2,1,0:T(8,128)} %bitcast.6, f32[1,128]{1,0:T(1,128)} %bitcast.7), custom_call_target="tpu_custom_call" | custom-call | tf_op jit(solution)/shard_map/pallas_call | solution.py:372
  227.3 2.3 copy.10
  229.6 2.3 copy.11
  (1 shorter events, 0.0 us)
Async XLA Ops:
  1.5 1.4 copy-start

commit v3 on v2

--- a/solution.py
+++ b/solution.py
@@ -25,7 +25,7 @@
     n, X, SB,
     slots, prev, last, blocks_hbm, right, lam,
     sol, res,
-    blocks, panel, img, imr, chain, acc, xs, xr, zs, zr, es, er, p, q, all_buf,
+    blocks, panel, img, imr, chain, acc, xs, xr, zs, zr, es, er, p, images, all_buf,
     blk_sem, agz_s, agz_r, agx_s, agx_r, age_s, age_r, ft_s, ft_r,
     rsx_s, rsx_r, rsz_s, rsz_r, rse_s, rse_r, ar_s, ar_r,
 ):
@@ -56,6 +56,7 @@
         )
 
     HS = SB // 2
+    zero = jnp.zeros((8, right.shape[-1]), F32)
     zp = z + 1 - 2 * (z % 2)
     peer = me + X - 2 * X * (z % 2)
 
@@ -65,7 +66,7 @@
     def piece(t, xx, h):
         return panel.at[pl.ds((t * X + xx) * SB + h * HS, HS)]
 
-    def gather(it):
+    def gather(it, beside=None):
         def zcopy(t, h, d):
             return to(piece(t, x, h), piece(t, x, h), agz_s.at[it, d, t, h],
                       agz_r.at[it, t, h], samples=me + (X if d == 0 else -X))
@@ -87,6 +88,8 @@
                 pl.when((z + 1 < Z) if d == 0 else (z > 0))(
                     lambda h=h, d=d: zcopy(z, h, d).start())
             send_x(z, h)
+        if beside is not None:
+            beside()
         for k in range(1, Z):
             for h in (0, 1):
                 for d in (0, 1):
@@ -101,7 +104,7 @@
                             pl.when(t != zp)(lambda: send_x(t, h))
                         else:
                             send_x(t, h)
-            if k == 1:
+            if k == max(Z - 2, 1):
                 for dx in range(1, X):
                     xcopy(z, 1, dx, (x - dx + X) % X).wait_recv()
                     ecopy(z, dx).start()
@@ -122,7 +125,7 @@
         for dx in range(1, X):
             ecopy(z, dx).wait_send()
 
-    def products(it):
+    def products(it, ratio_of=None):
         def part(c):
             rows = pl.ds(c * CH, CH)
             return to(img.at[rows], imr.at[rows], ft_s.at[it, c], ft_r.at[it, c],
@@ -140,15 +143,23 @@
                     img[r] = jnp.dot(lhs, rhs, preferred_element_type=F32)
 
             part(c).start()
+        ratio = None if ratio_of is None else ratio_of()
+        squares = zero
         for c in range(RB // CH):
             part(c).wait_recv()
 
-            @pl.loop(c * CH, (c + 1) * CH, step=U)
-            def _(r0):
+            def back(g, squares):
+                r0 = c * CH + g * U
                 terms = []
                 for u in range(U):
                     r = r0 + u
-                    narrow = (img[r] + imr[r]).astype(BF16)
+                    image = img[r] + imr[r]
+                    if ratio is not None:
+                        image = image + ratio * images[r]
+                    if it < ITERS - 1:
+                        images[r] = image
+                    squares = squares + fold(image * image)
+                    narrow = image.astype(BF16)
                     wide = jnp.concatenate([blocks[r, e] for e in range(E)], axis=1)
                     terms.append(lax.dot_general(
                         wide, narrow, (((0,), (0,)), ((), ())), preferred_element_type=F32))
@@ -156,9 +167,13 @@
                     for e in range(E):
                         i = (r0 + u) * E + e
                         chain[i + 1] = terms[u][e * B:(e + 1) * B] + chain[prev[i]]
+                return squares
+
+            squares = lax.fori_loop(0, CH // U, back, squares)
 
         for c in range(RB // CH):
             part(c).wait_send()
+        return jnp.where(core == 0, squares, zero), ratio
 
     def scatter(it):
         def xcopy(t, h, dx):
@@ -269,83 +284,86 @@
         for dx in range(1, X):
             ecopy(dx).wait_send()
 
-    def all_sum(j, values):
-        m = len(values)
+    def tile_copy(j, m, d, src):
+        other = (mine + d) % (2 * n)
         rows = pl.ds(0, 8 * m)
+        return to(all_buf.at[j, src, rows], all_buf.at[j, src, rows], ar_s.at[j, d],
+                  ar_r.at[j, d], samples=other // 2, features=other % 2)
+
+    def sum_start(j, values):
         for i, v in enumerate(values):
             all_buf[j, mine, pl.ds(8 * i, 8)] = v
 
-        def copy(d, src):
-            other = (mine + d) % (2 * n)
-            return to(all_buf.at[j, src, rows], all_buf.at[j, src, rows], ar_s.at[j, d],
-                      ar_r.at[j, d], samples=other // 2, features=other % 2)
-
         @pl.loop(1, 2 * n)
         def _(d):
-            copy(d, mine).start()
-
+            tile_copy(j, len(values), d, mine).start()
+
+    def sum_finish(j, m):
         @pl.loop(1, 2 * n)
         def _(d):
-            copy(d, (mine - d + 2 * n) % (2 * n)).wait_recv()
+            tile_copy(j, m, d, (mine - d + 2 * n) % (2 * n)).wait_recv()
 
         @pl.loop(1, 2 * n)
         def _(d):
-            copy(d, mine).wait_send()
-
+            tile_copy(j, m, d, mine).wait_send()
+
+        rows = pl.ds(0, 8 * m)
         total = all_buf[j, 0, rows]
         for s in range(1, 2 * n):
             total = total + all_buf[j, s, rows]
         return [jnp.sum(total[8 * i:8 * i + 8], axis=0, keepdims=True) for i in range(m)]
 
-    zero = jnp.zeros((8, right.shape[-1]), F32)
     for w in range(SB):
         panel[me * SB + w] = right[w].astype(BF16)
     pl.semaphore_wait(barrier, 2 * n - 1)
     gather(0)
     chain[0] = jnp.zeros(chain.shape[1:], F32)
     load.wait()
-    norm = None
+    norm = norm_next = None
     for it in range(ITERS):
-        final = it == ITERS - 1
-        direction = right if it == 0 else p
-        residual = right if it == 0 else res
-        products(it)
-        scatter(it)
-
-        def curve(w, carry):
-            dot, sq = carry
-            v = direction[w]
-            image = acc[z, w] + lam[...] * v
-            q[w] = image
-            return dot + fold(v * image), sq + fold(v * v)
-
-        dot, sq = lax.fori_loop(0, SB, curve, (zero, zero))
-        if it == 0:
-            norm, curvature = all_sum(0, [sq, dot])
+        first, final = it == 0, it == ITERS - 1
+        direction = right if first else p
+        residual = right if first else res
+
+        if first:
+            squares, _ = products(it)
+            own = lax.fori_loop(0, SB, lambda w, c: c + fold(right[w] * right[w]), zero)
+            sum_start(0, [own, squares + lam[...] * own])
+            scatter(it)
+            norm, curvature = sum_finish(0, 2)
         else:
-            (curvature,) = all_sum(2 * it, [dot])
+            def ratio_of():
+                nonlocal norm, norm_next
+                (norm_next,) = sum_finish(2 * it - 1, 1)
+                return norm_next / norm
+
+            squares, ratio = products(it, ratio_of)
+            norm = norm_next
+            before = right if it == 1 else p
+
+            def turn(w, carry):
+                v = res[w] + ratio * before[w]
+                p[w] = v
+                return carry + fold(v * v)
+
+            own = lax.fori_loop(0, SB, turn, zero)
+            sum_start(2 * it, [squares + lam[...] * own])
+            scatter(it)
+            (curvature,) = sum_finish(2 * it, 1)
         step = norm / curvature
 
         def update(w, carry):
             v = direction[w]
-            sol[w] = step * v if it == 0 else sol[w] + step * v
-            new = residual[w] - step * q[w]
+            sol[w] = step * v if first else sol[w] + step * v
+            new = residual[w] - step * (acc[z, w] + lam[...] * v)
             res[w] = new
+            if not final:
+                panel[me * SB + w] = new.astype(BF16)
             return carry + fold(new * new)
 
         sq = lax.fori_loop(0, SB, update, zero)
         if not final:
-            (norm_next,) = all_sum(2 * it + 1, [sq])
-            ratio = norm_next / norm
-            norm = norm_next
-
-            @pl.loop(0, SB)
-            def _(w):
-                v = res[w] + ratio * direction[w]
-                p[w] = v
-                panel[me * SB + w] = v.astype(BF16)
-
-            gather(it + 1)
+            gather(it + 1, lambda: sum_start(2 * it + 1, [sq]))
 
 
 def img_chunks(rb):
@@ -388,7 +406,7 @@
             pltpu.VMEM((X - 1, SB // 2, B, K), BF16),
             pltpu.VMEM((X - 1, SB // 2, B, K), BF16),
             pltpu.VMEM((SB, B, K), F32),
-            pltpu.VMEM((SB, B, K), F32),
+            pltpu.VMEM((RB, B, K), F32),
             pltpu.VMEM((J, 2 * n, 16, K), F32),
             dma,
             dma((ITERS, 2, Z, 2)), dma((ITERS, Z, 2)),

time: 232 us -> 211 us (0.909)
  Pallas kernels: 224 us -> 203 us
    pallas_call x1, Pallas kernels: 224 us -> 203 us  [per_device(): pl.pallas_call(functools.partial(kernel, n, X, SB), out_shape=[jax.ShapeD...]
where the time goes in v3:
time: 211 us; the launch traced here: 210 us
  Pallas kernels  203 us (96%)
  local copies, waits for them, and re-layouts  4.74 us (2%)
    pallas_call x1, Pallas kernels, per_device(): pl.pallas_call(functools.partial(kernel, n, X, SB), out_shape=[jax.ShapeD...  203 us
    unnamed x4, local copies, waits for them, and re-layouts  4.53 us

profile of v3, /device:TPU:0, one launch (start us, length us, event | category | flops | bytes accessed | tf_op | source)
XLA Modules:
  0.0 210.5 jit_solution(13369599750871074849)
XLA Ops:
  0.6 0.7 fusion.3
  1.3 0.1 copy.7
  1.4 0.1 reshape.26.slots
  1.5 0.0 copy-start
  1.6 0.6 select_reduce_fusion.1.last
  2.2 0.7 select_reduce_fusion.prev
  3.0 0.0 copy-done
  3.0 203.0 %shard_map.59 = (f32[16,128,128]{2,1,0:T(8,128)}, f32[16,128,128]{2,1,0:T(8,128)}) custom-call(s32[180]{0:T(256)} %copy-done, s32[180]{0:T(256)} %select_reduce_fusion.prev, s32[128]{0:T(128)} %select_reduce_fusion.1.last, bf16[45,4,128,128]{3,2,1,0:T(8,128)(2,1)} %blocks_hbm.1, f32[16,128,128]{2,1,0:T(8,128)} %bitcast.6, f32[1,128]{1,0:T(1,128)} %bitcast.7), custom_call_target="tpu_custom_call" | custom-call | tf_op jit(solution)/shard_map/pallas_call | solution.py:390
  205.9 2.3 %copy.10 = f32[2048,128]{1,0:T(8,128)} copy(f32[2048,128]{1,0:T(8,128)} %bitcast.5) | data formatting | bytes 2097152
  208.2 2.3 %copy.11 = f32[2048,128]{1,0:T(8,128)} copy(f32[2048,128]{1,0:T(8,128)} %bitcast.4) | data formatting | bytes 2097152
  (1 shorter events, 0.0 us)
Async XLA Ops:
  1.5 1.4 copy-start

commit v4 on v3

--- a/solution.py
+++ b/solution.py
@@ -31,7 +31,7 @@
 ):
     Z = n // X
     RB, E, B = blocks.shape[:3]
-    CH = RB // img_chunks(RB)
+    CH = img_rows(RB)
     me = lax.axis_index("samples")
     core = lax.axis_index("features")
     z, x = me // X, me % X
@@ -66,7 +66,7 @@
     def piece(t, xx, h):
         return panel.at[pl.ds((t * X + xx) * SB + h * HS, HS)]
 
-    def gather(it, beside=None):
+    def gather(it, beside, late):
         def zcopy(t, h, d):
             return to(piece(t, x, h), piece(t, x, h), agz_s.at[it, d, t, h],
                       agz_r.at[it, t, h], samples=me + (X if d == 0 else -X))
@@ -88,8 +88,7 @@
                 pl.when((z + 1 < Z) if d == 0 else (z > 0))(
                     lambda h=h, d=d: zcopy(z, h, d).start())
             send_x(z, h)
-        if beside is not None:
-            beside()
+        beside()
         for k in range(1, Z):
             for h in (0, 1):
                 for d in (0, 1):
@@ -108,6 +107,7 @@
                 for dx in range(1, X):
                     xcopy(z, 1, dx, (x - dx + X) % X).wait_recv()
                     ecopy(z, dx).start()
+        late()
         for t in range(Z):
             for dx in range(1, X):
                 xcopy(t, 0, dx, (x - dx + X) % X).wait_recv()
@@ -115,67 +115,70 @@
                     lambda t=t, dx=dx: xcopy(t, 1, dx, (x - dx + X) % X).wait_recv())
         for dx in range(1, X):
             ecopy(zp, dx).wait_recv()
-        for t in range(Z):
-            for dx in range(1, X):
-                xcopy(t, 0, dx, x).wait_send()
-                pl.when(t != zp)(lambda t=t, dx=dx: xcopy(t, 1, dx, x).wait_send())
-            for h in (0, 1):
-                pl.when((t <= z) & (z + 1 < Z))(lambda t=t, h=h: zcopy(t, h, 0).wait_send())
-                pl.when((t >= z) & (z > 0))(lambda t=t, h=h: zcopy(t, h, 1).wait_send())
-        for dx in range(1, X):
-            ecopy(z, dx).wait_send()
-
-    def products(it, ratio_of=None):
+
+        def drain():
+            for t in range(Z):
+                for dx in range(1, X):
+                    xcopy(t, 0, dx, x).wait_send()
+                    pl.when(t != zp)(lambda t=t, dx=dx: xcopy(t, 1, dx, x).wait_send())
+                for h in (0, 1):
+                    pl.when((t <= z) & (z + 1 < Z))(
+                        lambda t=t, h=h: zcopy(t, h, 0).wait_send())
+                    pl.when((t >= z) & (z > 0))(
+                        lambda t=t, h=h: zcopy(t, h, 1).wait_send())
+            for dx in range(1, X):
+                ecopy(z, dx).wait_send()
+
+        return drain
+
+    def products(it, ratio, drain):
         def part(c):
             rows = pl.ds(c * CH, CH)
             return to(img.at[rows], imr.at[rows], ft_s.at[it, c], ft_r.at[it, c],
                       features=1 - core)
 
-        U = 3 if CH % 3 == 0 else 1
-
-        for c in range(RB // CH):
-            @pl.loop(c * CH, (c + 1) * CH, step=U)
-            def _(r0):
-                for u in range(U):
-                    r = r0 + u
-                    lhs = jnp.concatenate([blocks[r, e] for e in range(E)], axis=1)
-                    rhs = jnp.concatenate([panel[slots[r * E + e]] for e in range(E)], axis=0)
-                    img[r] = jnp.dot(lhs, rhs, preferred_element_type=F32)
-
+        @pl.loop(0, RB // CH)
+        def _(c):
+            for u in range(CH):
+                r = c * CH + u
+                lhs = jnp.concatenate([blocks[r, e] for e in range(E)], axis=1)
+                rhs = jnp.concatenate([panel[slots[r * E + e]] for e in range(E)], axis=0)
+                img[r] = jnp.dot(lhs, rhs, preferred_element_type=F32)
             part(c).start()
-        ratio = None if ratio_of is None else ratio_of()
-        squares = zero
-        for c in range(RB // CH):
+
+        drain()
+
+        def back(c, squares):
             part(c).wait_recv()
-
-            def back(g, squares):
-                r0 = c * CH + g * U
-                terms = []
-                for u in range(U):
-                    r = r0 + u
-                    image = img[r] + imr[r]
-                    if ratio is not None:
-                        image = image + ratio * images[r]
-                    if it < ITERS - 1:
-                        images[r] = image
-                    squares = squares + fold(image * image)
-                    narrow = image.astype(BF16)
-                    wide = jnp.concatenate([blocks[r, e] for e in range(E)], axis=1)
-                    terms.append(lax.dot_general(
-                        wide, narrow, (((0,), (0,)), ((), ())), preferred_element_type=F32))
-                for u in range(U):
-                    for e in range(E):
-                        i = (r0 + u) * E + e
-                        chain[i + 1] = terms[u][e * B:(e + 1) * B] + chain[prev[i]]
-                return squares
-
-            squares = lax.fori_loop(0, CH // U, back, squares)
-
-        for c in range(RB // CH):
-            part(c).wait_send()
-        return jnp.where(core == 0, squares, zero), ratio
-
-    def scatter(it):
+            terms = []
+            for u in range(CH):
+                r = c * CH + u
+                image = img[r] + imr[r]
+                if ratio is not None:
+                    image = image + ratio * images[r]
+                if it < ITERS - 1:
+                    images[r] = image
+                squares = squares + fold(image * image)
+                narrow = image.astype(BF16)
+                wide = jnp.concatenate([blocks[r, e] for e in range(E)], axis=1)
+                terms.append(lax.dot_general(
+                    wide, narrow, (((0,), (0,)), ((), ())), preferred_element_type=F32))
+            for u in range(CH):
+                for e in range(E):
+                    i = (c * CH + u) * E + e
+                    chain[i + 1] = terms[u][e * B:(e + 1) * B] + chain[prev[i]]
+            return squares
+
+        squares = lax.fori_loop(0, RB // CH, back, zero)
+
+        def sent():
+            @pl.loop(0, RB // CH)
+            def _(c):
+                part(c).wait_send()
+
+        return jnp.where(core == 0, squares, zero), sent
+
+    def scatter(it, beside, late):
         def xcopy(t, h, dx):
             return to(xs.at[dx - 1, t, half(h)], xr.at[dx - 1, t, half(h)],
                       rsx_s.at[it, dx - 1, t, h], rsx_r.at[it, dx - 1, t, h],
@@ -238,6 +241,8 @@
             def _(w):
                 acc[t, w] = term(t, x, w)
 
+        beside()
+
         def add_x(t, h):
             for dx in range(1, X):
                 xcopy(t, h, dx).wait_recv()
@@ -257,6 +262,8 @@
                 acc[t, w] = acc[t, w] + zr[d, t, w].astype(F32)
 
         for k, t in enumerate(order):
+            if k == Z - 1:
+                late()
             for h in (0, 1):
                 if h == 1 and k < Z - 1:
                     pl.when(t != zp)(lambda t=t: add_x(t, 1))
@@ -275,14 +282,17 @@
                     zs[t, w] = acc[t, w].astype(BF16)
 
                 zcopy(t, h, d).start()
-        for t in range(Z):
-            for dx in range(1, X):
-                xcopy(t, 0, dx).wait_send()
-                pl.when(t != zp)(lambda t=t, dx=dx: xcopy(t, 1, dx).wait_send())
-            for h in (0, 1):
-                pl.when(t != z)(lambda t=t, h=h: zcopy(t, h, 0).wait_send())
-        for dx in range(1, X):
-            ecopy(dx).wait_send()
+        def drain():
+            for t in range(Z):
+                for dx in range(1, X):
+                    xcopy(t, 0, dx).wait_send()
+                    pl.when(t != zp)(lambda t=t, dx=dx: xcopy(t, 1, dx).wait_send())
+                for h in (0, 1):
+                    pl.when(t != z)(lambda t=t, h=h: zcopy(t, h, 0).wait_send())
+            for dx in range(1, X):
+                ecopy(dx).wait_send()
+
+        return drain
 
     def tile_copy(j, m, d, src):
         other = (mine + d) % (2 * n)
@@ -313,44 +323,48 @@
             total = total + all_buf[j, s, rows]
         return [jnp.sum(total[8 * i:8 * i + 8], axis=0, keepdims=True) for i in range(m)]
 
-    for w in range(SB):
+    @pl.loop(0, SB)
+    def _(w):
         panel[me * SB + w] = right[w].astype(BF16)
+
     pl.semaphore_wait(barrier, 2 * n - 1)
-    gather(0)
     chain[0] = jnp.zeros(chain.shape[1:], F32)
-    load.wait()
-    norm = norm_next = None
+    got = {}
+
+    def first_norm():
+        got["own"] = lax.fori_loop(0, SB, lambda w, c: c + fold(right[w] * right[w]), zero)
+
+    gathered = gather(0, first_norm, load.wait)
+    norm = ratio = None
     for it in range(ITERS):
         first, final = it == 0, it == ITERS - 1
         direction = right if first else p
         residual = right if first else res
-
+        squares, sent = products(it, ratio, gathered)
+
+        def send_sums():
+            own = got["own"]
+            if first:
+                sum_start(0, [own, squares + lam[...] * own])
+            else:
+                before = right if it == 1 else p
+
+                def turn(w, carry):
+                    v = res[w] + ratio * before[w]
+                    p[w] = v
+                    return carry + fold(v * v)
+
+                own = lax.fori_loop(0, SB, turn, zero)
+                sum_start(2 * it, [squares + lam[...] * own])
+            sent()
+
+        def take_sums():
+            got["sums"] = sum_finish(2 * it, 2 if first else 1)
+
+        scattered = scatter(it, send_sums, take_sums)
         if first:
-            squares, _ = products(it)
-            own = lax.fori_loop(0, SB, lambda w, c: c + fold(right[w] * right[w]), zero)
-            sum_start(0, [own, squares + lam[...] * own])
-            scatter(it)
-            norm, curvature = sum_finish(0, 2)
-        else:
-            def ratio_of():
-                nonlocal norm, norm_next
-                (norm_next,) = sum_finish(2 * it - 1, 1)
-                return norm_next / norm
-
-            squares, ratio = products(it, ratio_of)
-            norm = norm_next
-            before = right if it == 1 else p
-
-            def turn(w, carry):
-                v = res[w] + ratio * before[w]
-                p[w] = v
-                return carry + fold(v * v)
-
-            own = lax.fori_loop(0, SB, turn, zero)
-            sum_start(2 * it, [squares + lam[...] * own])
-            scatter(it)
-            (curvature,) = sum_finish(2 * it, 1)
-        step = norm / curvature
+            norm = got["sums"][0]
+        step = norm / got["sums"][-1]
 
         def update(w, carry):
             v = direction[w]
@@ -362,12 +376,23 @@
             return carry + fold(new * new)
 
         sq = lax.fori_loop(0, SB, update, zero)
-        if not final:
-            gather(it + 1, lambda: sum_start(2 * it + 1, [sq]))
-
-
-def img_chunks(rb):
-    return max(d for d in range(1, 6) if rb % d == 0)
+        if final:
+            scattered()
+        else:
+            def send_norm():
+                sum_start(2 * it + 1, [sq])
+                scattered()
+
+            def take_norm():
+                got["norm"] = sum_finish(2 * it + 1, 1)[0]
+
+            gathered = gather(it + 1, send_norm, take_norm)
+            ratio = got["norm"] / norm
+            norm = got["norm"]
+
+
+def img_rows(rb):
+    return max(d for d in range(1, 4) if rb % d == 0)
 
 
 def per_device(n, blocks, block_cols, right_side, lambdas):
@@ -382,7 +407,7 @@
     prev = jnp.max(jnp.where(same, entries[None, :] + 1, 0), axis=1)
     hit = slots[None, :] == jnp.arange(n * SB, dtype=jnp.int32)[:, None]
     last = jnp.max(jnp.where(hit, entries[None, :] + 1, 0), axis=1)
-    C = img_chunks(RB)
+    C = RB // img_rows(RB)
     dma = pltpu.SemaphoreType.DMA
     J = 2 * ITERS
     smem = pl.BlockSpec(memory_space=pltpu.SMEM)

time: 211 us -> 210 us (level)
  no operation moved by 1% of the time
where the time goes in v4:
time: 210 us; the launch traced here: 209 us
  Pallas kernels  202 us (96%)
  local copies, waits for them, and re-layouts  4.74 us (2%)
  other arithmetic  2.1 us (1%)
    pallas_call x1, Pallas kernels, per_device(): pl.pallas_call(functools.partial(kernel, n, X, SB), out_shape=[jax.ShapeD...  202 us
    unnamed x4, local copies, waits for them, and re-layouts  4.53 us

profile of v4, /device:TPU:0, one launch (start us, length us, event | category | flops | bytes accessed | tf_op | source)
XLA Modules:
  0.0 209.3 jit_solution(17972639415283734587)
XLA Ops:
  0.6 0.7 fusion.3
  1.3 0.1 copy.7
  1.4 0.1 reshape.26.slots
  1.5 0.0 copy-start
  1.6 0.6 select_reduce_fusion.1.last
  2.2 0.7 select_reduce_fusion.prev
  3.0 0.0 copy-done
  3.0 201.8 %shard_map.59 = (f32[16,128,128]{2,1,0:T(8,128)}, f32[16,128,128]{2,1,0:T(8,128)}) custom-call(s32[180]{0:T(256)} %copy-done, s32[180]{0:T(256)} %select_reduce_fusion.prev, s32[128]{0:T(128)} %select_reduce_fusion.1.last, bf16[45,4,128,128]{3,2,1,0:T(8,128)(2,1)} %blocks_hbm.1, f32[16,128,128]{2,1,0:T(8,128)} %bitcast.6, f32[1,128]{1,0:T(1,128)} %bitcast.7), custom_call_target="tpu_custom_call" | custom-call | tf_op jit(solution)/shard_map/pallas_call | solution.py:415
  204.8 2.3 %copy.10 = f32[2048,128]{1,0:T(8,128)} copy(f32[2048,128]{1,0:T(8,128)} %bitcast.5) | data formatting | bytes 2097152
  207.0 2.3 %copy.11 = f32[2048,128]{1,0:T(8,128)} copy(f32[2048,128]{1,0:T(8,128)} %bitcast.4) | data formatting | bytes 2097152
  (1 shorter events, 0.0 us)
Async XLA Ops:
  1.5 1.4 copy-start
